TPU v7x, 32 devices: a whole 2x2x4 slice. The times are simulated.
32 devices in a mesh: diff: 16 (over z, x, core), obj: 2 (over y).
Axes of the slice: x: 2, y: 2, z: 4, core: 2. Of those that a mesh axis runs over, the one named last changes fastest.
Arguments:
- object_field: float32 [2, 4096, 512], P(None, ('diff', 'obj')), may hold values from -6 to 6
- probe_modes: float32 [4, 2, 256, 256], P('obj'), may hold values from -3 to 3
- amplitudes: float32 [32, 256, 256], P('diff')
- offsets: int32 [32, 2], P('diff'), may hold values from 0 to 256, as said below
- counts: int32 [16], replicated, may hold values from 1 to 2, as said below
Outputs:
- object_out: float32 [2, 4096, 512], P(None, ('diff', 'obj'))
- probe_out: float32 [4, 2, 256, 256], P('obj')
Inputs may be any that keep to these rules, and one draw needn't show every extreme that they name: Row k of offsets holds the block-local corner of slot k (block k // 2): offsets[k,0] < 256, and offsets[k,0] <= 0 in the last block; offsets[k,1] <= 256. Every slot, used or not, holds such a corner. Block b uses its first counts[b] slots.
All inputs are finite; a program needn't handle non-finite values.
Results may differ from a plain program's by a relative error of at most 0.0003.
Values sent between devices are 32-bit elements; how exact they have to be, the bound alone decides.
A program may use at most 64 MiB of HBM per device.

v0:
```python
import functools

import jax
import jax.numpy as jnp
import ml_dtypes
import numpy as np
from jax import lax
from jax.experimental import pallas as pl
from jax.experimental.pallas import tpu as pltpu
from jax.sharding import PartitionSpec as P

PASSES = 3
EDGE_SCALE = 1.0
DIFFUSION_RATE = 0.2
OBJECT_STEP = 0.25
EDGE = 8
MESH = pl.DeviceIdType.MESH
BF16 = jnp.bfloat16
F32 = jnp.float32


def dft_blocks(length):
    ladder = np.arange(length)
    angle = (ladder[:, None] * ladder[None, :] % length) * (2.0 * np.pi / length)
    cosine = np.cos(angle) / np.sqrt(length)
    sine = np.sin(angle) / np.sqrt(length)
    forward = np.block([[cosine, sine], [-sine, cosine]]).astype(np.float32)

    def halves(table):
        high = table.astype(ml_dtypes.bfloat16)
        low = (table - high.astype(np.float32)).astype(ml_dtypes.bfloat16)
        return np.stack([high, low])

    return np.stack([halves(forward), halves(forward.T)])


def split(value):
    high = value.astype(BF16)
    return high, (value - high.astype(F32)).astype(BF16)


def dot(a, b):
    return jnp.dot(a, b, preferred_element_type=F32)


def transform(real, imag, tables, left, right, length):
    high, low = split(jnp.concatenate([real, imag], axis=0))
    mid = dot(tables[left, 0], high) + dot(tables[left, 0], low) + dot(tables[left, 1], high)
    high, low = split(jnp.concatenate([mid[:length], mid[length:]], axis=1))
    out = dot(high, tables[right, 0]) + dot(low, tables[right, 0]) + dot(high, tables[right, 1])
    return out


def flux_of(real, imag):
    weight = 1.0 / (1.0 + (real * real + imag * imag) / (EDGE_SCALE * EDGE_SCALE))
    return real * weight, imag * weight


def kernel(n, obj_ref, probe_ref, amp_ref, off_ref, cnt_ref, tab_ref, out_ref, pout_ref,
           ext, pf, far, pw, pw_in, gext, patch, spill, ysend, yin, mar, ps, rbuf, po, ssem, rsem):
    tile, columns = obj_ref.shape[1:]
    length = pf.shape[-1]
    slots, modes = pf.shape[0], probe_ref.shape[0]
    block = 2 * tile
    bits = n.bit_length() - 1
    d, o = lax.axis_index("diff"), lax.axis_index("obj")
    q = 1 - o
    has_low, has_high = d > 0, d < n - 1
    rank = 2 * d + o
    has_prev, has_next = rank > 0, rank < 2 * n - 1
    partner = {"diff": d, "obj": q}
    lower = {"diff": d - 1, "obj": o}
    upper = {"diff": d + 1, "obj": o}
    prev_tile = {"diff": d - 1 + o, "obj": q}
    next_tile = {"diff": d + o, "obj": q}
    bit = [lax.rem(d // (1 << k), 2) for k in range(bits)]
    cube = [{"diff": d + (1 - 2 * bit[k]) * (1 << k), "obj": o} for k in range(bits)]

    def remote(src, dst, index, device):
        return pltpu.make_async_remote_copy(
            src_ref=src, dst_ref=dst, send_sem=ssem.at[index], recv_sem=rsem.at[index],
            device_id=device, device_id_type=MESH)

    def rows(start, size):
        return pl.ds(pl.multiple_of(start, 8), size)

    def pick(shape, long, offset):
        far_at = lax.broadcasted_iota(jnp.int32, shape, long)
        near_at = lax.broadcasted_iota(jnp.int32, shape, 1 - long)
        return jnp.where(far_at - near_at == offset, 1.0, 0.0).astype(BF16)

    barrier = pltpu.get_barrier_semaphore()

    def greet(device):
        pl.semaphore_signal(barrier, inc=1, device_id=device, device_id_type=MESH)

    greet(partner)
    for k in range(bits):
        greet(cube[k])
    other = d - 1 + 2 * bit[0]
    cross = d - 1 + 2 * o
    has_other = (other >= 0) & (other < n)
    has_cross = (cross >= 0) & (cross < n)

    @pl.when(has_other)
    def _():
        greet({"diff": other, "obj": o})

    @pl.when(has_cross)
    def _():
        greet({"diff": cross, "obj": q})

    pl.semaphore_wait(barrier, 1 + bits + has_other.astype(jnp.int32) + has_cross.astype(jnp.int32))

    to_partner, direct, relay = [], [], []
    for c in range(2):
        to_partner.append(remote(obj_ref.at[c], ext.at[c, rows(o * tile, tile)], c, partner))
        direct.append(remote(obj_ref.at[c], ext.at[c, rows(block + o * tile, tile)], 2 + c, lower))
        relay.append(remote(ext.at[c, rows(q * tile, tile)], ext.at[c, rows(block + q * tile, tile)], 4 + c, lower))
        to_partner[c].start()
    for c in range(2):
        pl.when(has_low)(direct[c].start)
    for c in range(2):
        ext[c, rows(o * tile, tile), :] = obj_ref[c]

    @pl.when(d == n - 1)
    def _():
        for c in range(2):
            ext[c, block:, :] = jnp.zeros((block, columns), F32)

    @pl.when(d == 0)
    def _():
        spill[...] = jnp.zeros_like(spill)

    @pl.when(rank == 0)
    def _():
        mar[:, :EDGE, :] = jnp.zeros((2, EDGE, columns), F32)

    @pl.when(rank == 2 * n - 1)
    def _():
        mar[:, EDGE + tile:, :] = jnp.zeros((2, EDGE, columns), F32)

    for c in range(2):
        to_partner[c].wait_recv()
        pl.when(has_low)(relay[c].start)
    for c in range(2):
        pl.when(has_high)(direct[c].wait_recv)
    for c in range(2):
        pl.when(has_high)(relay[c].wait_recv)

    power_copy = []
    for s in range(slots):
        row_pick = pick((length, 2 * block), 1, off_ref[s, 0])
        column_pick = pick((columns, length), 0, off_ref[s, 1])
        for c in range(2):
            high, low = split(ext[c])
            high, low = split(dot(high, column_pick) + dot(low, column_pick))
            pf[s, c] = dot(row_pick, high) + dot(row_pick, low)
        pw[s] = jnp.zeros((length, length), F32)

        @pl.loop(0, modes)
        def _(m, s=s):
            pr, pi = probe_ref[m, 0], probe_ref[m, 1]
            fr, fi = pf[s, 0], pf[s, 1]
            wave = transform(pr * fr - pi * fi, pr * fi + pi * fr, tab_ref, 0, 1, length)
            far[s, m] = wave
            real, imag = wave[:, :length], wave[:, length:]
            pw[s] += real * real + imag * imag

        power_copy.append(remote(pw.at[s], pw_in.at[s], 6 + s, partner))
        power_copy[s].start()

    base = 6 + slots
    for s in range(slots):
        used = jnp.full((1, length), cnt_ref[d], jnp.int32)
        weight = jnp.where(used > s, 1.0, 0.0).astype(F32)
        power_copy[s].wait_recv()
        patch[...] = jnp.zeros_like(patch)
        pw_in[s] = amp_ref[s] / jnp.sqrt(pw[s] + pw_in[s] + 1.0) - 1.0

        @pl.loop(0, modes)
        def _(m, s=s, weight=weight):
            pr, pi = probe_ref[m, 0], probe_ref[m, 1]
            fr, fi = pf[s, 0], pf[s, 1]
            factor = pw_in[s]
            back = transform(far[s, m, :, :length] * factor, far[s, m, :, length:] * factor,
                             tab_ref, 1, 0, length)
            real, imag = back[:, :length] * weight, back[:, length:] * weight
            patch[0] += pr * real + pi * imag
            patch[1] += pr * imag - pi * real
            grad_r = fr * real + fi * imag
            grad_i = fr * imag - fi * real
            at_r = rows(m * 2 * length, length)
            at_i = rows(m * 2 * length + length, length)
            if s == 0:
                ps[at_r, :] = grad_r
                ps[at_i, :] = grad_i
            else:
                ps[at_r, :] += grad_r
                ps[at_i, :] += grad_i

        row_place = pick((2 * block, length), 0, off_ref[s, 0])
        column_place = pick((length, columns), 1, off_ref[s, 1])
        for c in range(2):
            high, low = split(patch[c])
            high, low = split(dot(row_place, high) + dot(row_place, low))
            placed = dot(high, column_place) + dot(low, column_place)
            if s == 0:
                gext[c] = placed
            else:
                gext[c] += placed

    spill_copy = [remote(gext.at[:, rows(block + t * tile, tile)], spill.at[h], base + h, upper)
                  for h, t in ((0, q), (1, o))]
    for copy in spill_copy:
        pl.when(has_high)(copy.start)

    sums_at, share_at = base + 5, base + 5 + bits
    total = ps.shape[0]
    starts, sizes = [jnp.int32(0)], [total]
    sums, shares = [], []
    filled = 0
    for k in range(bits):
        half = sizes[k] // 2
        sums.append(remote(ps.at[rows(starts[k] + (1 - bit[k]) * half, half)], rbuf.at[pl.ds(filled, half)],
                           sums_at + k, cube[k]))
        starts.append(starts[k] + bit[k] * half)
        sizes.append(half)
        filled += half
    for k in range(bits):
        mine = po.at[rows(starts[k + 1], sizes[k + 1])]
        shares.append(remote(mine, mine, share_at + k, cube[k]))

    def add_sum(k):
        sums[k].wait_recv()
        at = total - sizes[k]
        keep = rows(starts[k + 1], sizes[k + 1])
        ps[keep, :] += rbuf[at:at + sizes[k + 1], :]

    sums[0].start()
    pl.when(has_low)(spill_copy[0].wait_recv)
    ysend[...] = gext[:, rows(q * tile, tile), :] + spill[0]
    to_owner = remote(ysend, yin, base + 2, partner)
    to_owner.start()
    for k in range(bits):
        add_sum(k)
        if k + 1 < bits:
            sums[k + 1].start()
    last = rows(starts[bits], sizes[bits])
    po[last, :] = ps[last, :]
    shares[bits - 1].start()

    pl.when(has_low)(spill_copy[1].wait_recv)
    to_owner.wait_recv()
    mar[:, EDGE:EDGE + tile, :] = obj_ref[...] + OBJECT_STEP * (gext[:, rows(o * tile, tile), :] + spill[1] + yin[...])
    up = remote(mar.at[:, pl.ds(EDGE, EDGE)], mar.at[:, pl.ds(EDGE + tile, EDGE)], base + 3, prev_tile)
    down = remote(mar.at[:, pl.ds(tile, EDGE)], mar.at[:, pl.ds(0, EDGE)], base + 4, next_tile)
    pl.when(has_prev)(up.start)
    pl.when(has_next)(down.start)
    left = list(range(bits - 1, -1, -1))

    def share():
        if left:
            k = left.pop(0)
            shares[k].wait_recv()
            if left:
                shares[left[0]].start()

    share()
    pl.when(has_next)(up.wait_recv)
    pl.when(has_prev)(down.wait_recv)

    tall = tile + 2 * EDGE
    ids = rank * tile - EDGE + lax.broadcasted_iota(jnp.int32, (tall, columns), 0)
    below = (ids >= 0) & (ids + 1 < 2 * n * tile)
    beside = lax.broadcasted_iota(jnp.int32, (tall, columns), 1) < columns - 1
    u_r, u_i = mar[0], mar[1]
    for sweep in range(PASSES):
        v_r, v_i = flux_of(pltpu.roll(u_r, tall - 1, 0) - u_r, pltpu.roll(u_i, tall - 1, 0) - u_i)
        h_r, h_i = flux_of(pltpu.roll(u_r, columns - 1, 1) - u_r, pltpu.roll(u_i, columns - 1, 1) - u_i)

        def moved(v, h):
            v = jnp.where(below, v, 0.0)
            h = jnp.where(beside, h, 0.0)
            return DIFFUSION_RATE * ((v - pltpu.roll(v, 1, 0)) + (h - pltpu.roll(h, 1, 1)))

        u_r, u_i = u_r + moved(v_r, h_r), u_i + moved(v_i, h_i)
        share()
    out_ref[0] = u_r[EDGE:EDGE + tile]
    out_ref[1] = u_i[EDGE:EDGE + tile]
    while left:
        share()
    for m in range(modes):
        for c in range(2):
            at = (m * 2 + c) * length
            pout_ref[m, c] = probe_ref[m, c] + po[at:at + length, :] / n

    for copy in to_partner + power_copy + sums + shares + [to_owner]:
        copy.wait_send()
    for copy in direct + relay:
        pl.when(has_low)(copy.wait_send)
    for copy in spill_copy:
        pl.when(has_high)(copy.wait_send)
    pl.when(has_prev)(up.wait_send)
    pl.when(has_next)(down.wait_send)


def body(n, object_field, probe_modes, amplitudes, offsets, counts):
    _, tile, columns = object_field.shape
    modes, _, length, _ = probe_modes.shape
    slots = amplitudes.shape[0]
    bits = n.bit_length() - 1
    block = 2 * tile
    copies = 11 + slots + 2 * bits
    vmem = pl.BlockSpec(memory_space=pltpu.VMEM)
    smem = pl.BlockSpec(memory_space=pltpu.SMEM)
    tables = jnp.asarray(dft_blocks(length))
    return pl.pallas_call(
        functools.partial(kernel, n),
        out_shape=(
            jax.ShapeDtypeStruct(object_field.shape, F32),
            jax.ShapeDtypeStruct(probe_modes.shape, F32),
        ),
        in_specs=[vmem, vmem, vmem, smem, smem, vmem],
        out_specs=(vmem, vmem),
        scratch_shapes=[
            pltpu.VMEM((2, 2 * block, columns), F32),
            pltpu.VMEM((slots, 2, length, length), F32),
            pltpu.VMEM((slots, modes, length, 2 * length), F32),
            pltpu.VMEM((slots, length, length), F32),
            pltpu.VMEM((slots, length, length), F32),
            pltpu.VMEM((2, 2 * block, columns), F32),
            pltpu.VMEM((2, length, length), F32),
            pltpu.VMEM((2, 2, tile, columns), F32),
            pltpu.VMEM((2, tile, columns), F32),
            pltpu.VMEM((2, tile, columns), F32),
            pltpu.VMEM((2, tile + 2 * EDGE, columns), F32),
            pltpu.VMEM((modes * 2 * length, length), F32),
            pltpu.VMEM((modes * 2 * length, length), F32),
            pltpu.VMEM((modes * 2 * length, length), F32),
            pltpu.SemaphoreType.DMA((copies,)),
            pltpu.SemaphoreType.DMA((copies,)),
        ],
        compiler_params=pltpu.CompilerParams(
            collective_id=0, has_side_effects=True, vmem_limit_bytes=48 * 2**20
        ),
    )(object_field, probe_modes, amplitudes, offsets, counts, tables)


def solution(mesh):
    placed = (
        P(None, ("diff", "obj"), None),
        P("obj", None, None, None),
        P("diff", None, None),
        P("diff", None),
        P(),
    )
    return jax.shard_map(
        functools.partial(body, mesh.shape["diff"]),
        mesh=mesh,
        in_specs=placed,
        out_specs=(P(None, ("diff", "obj"), None), P("obj", None, None, None)),
        check_vma=False,
    )
```

profile of v0, /device:TPU:1, one launch (start us, length us, event | category | flops | bytes accessed | tf_op | source)
XLA Modules:
  0.0 97.6 jit_solution(11017952779453746655)
XLA Ops:
  0.6 0.0 copy-start
  0.6 1.6 %copy-done = bf16[2,2,512,512]{3,2,1,0:T(8,128)(2,1)S(1)} copy-done((bf16[2,2,512,512]{3,2,1,0:T(8,128)(2,1)S(1)}, bf16[2,2,512,512]{3,2,1,0:T(8,128)(2,1)}, u32[]{:S(2)}) %copy-start) | copy-done | bytes 2097176
  2.2 0.0 copy-start.1
  2.2 1.2 %copy-done.1 = f32[2,2,256,256]{3,2,1,0:T(8,128)S(1)} copy-done((f32[2,2,256,256]{3,2,1,0:T(8,128)S(1)}, f32[2,2,256,256]{3,2,1,0:T(8,128)}, u32[]{:S(2)}) %copy-start.1) | copy-done | bytes 1048600
  3.5 0.0 copy-start.2
  3.5 1.0 %copy-done.2 = f32[2,128,512]{2,1,0:T(8,128)S(1)} copy-done((f32[2,128,512]{2,1,0:T(8,128)S(1)}, f32[2,128,512]{2,1,0:T(8,128)}, u32[]{:S(2)}) %copy-start.2) | copy-done | bytes 524312
  4.5 0.0 copy-start.3
  4.5 1.0 %copy-done.3 = f32[2,256,256]{2,1,0:T(8,128)S(1)} copy-done((f32[2,256,256]{2,1,0:T(8,128)S(1)}, f32[2,256,256]{2,1,0:T(8,128)}, u32[]{:S(2)}) %copy-start.3) | copy-done | bytes 524312
  5.5 0.0 copy-start.4
  5.5 0.7 copy-done.4
  6.2 0.0 copy-start.5
  6.2 0.7 copy-done.5
  6.9 89.0 %shard_map.77 = (f32[2,128,512]{2,1,0:T(8,128)S(1)}, f32[2,2,256,256]{3,2,1,0:T(8,128)S(1)}) custom-call(f32[2,128,512]{2,1,0:T(8,128)S(1)} %copy-done.2, f32[2,2,256,256]{3,2,1,0:T(8,128)S(1)} %copy-done.1, f32[2,256,256]{2,1,0:T(8,128)S(1)} %copy-done.3, s32[2,2]{1,0:T(2,128)S(1)} %copy-done.4, s32[16]{0:T(128)S(1)} %copy-done.5, ...), custom_call_target="tpu_custom_call" | custom-call | tf_op jit(solution)/shard_map/pallas_call | solution.py:318
  95.9 0.8 copy.10
  96.7 1.0 copy.11
Async XLA Ops:
  0.6 1.6 %copy-start = (bf16[2,2,512,512]{3,2,1,0:T(8,128)(2,1)S(1)}, bf16[2,2,512,512]{3,2,1,0:T(8,128)(2,1)}, u32[]{:S(2)}) copy-start(bf16[2,2,512,512]{3,2,1,0:T(8,128)(2,1)} %constant.2.clone.tab_ref) | copy-start | bytes 6291460
  2.2 1.2 %copy-start.1 = (f32[2,2,256,256]{3,2,1,0:T(8,128)S(1)}, f32[2,2,256,256]{3,2,1,0:T(8,128)}, u32[]{:S(2)}) copy-start(f32[2,2,256,256]{3,2,1,0:T(8,128)} %probe_ref.1) | copy-start | bytes 3145732
  3.5 1.0 %copy-start.2 = (f32[2,128,512]{2,1,0:T(8,128)S(1)}, f32[2,128,512]{2,1,0:T(8,128)}, u32[]{:S(2)}) copy-start(f32[2,128,512]{2,1,0:T(8,128)} %obj_ref.1) | copy-start | bytes 1572868
  4.5 1.0 %copy-start.3 = (f32[2,256,256]{2,1,0:T(8,128)S(1)}, f32[2,256,256]{2,1,0:T(8,128)}, u32[]{:S(2)}) copy-start(f32[2,256,256]{2,1,0:T(8,128)} %amp_ref.1) | copy-start | bytes 1572868
  5.5 0.7 copy-start.4
  6.2 0.7 copy-start.5
where the time goes:
time: 97.9 us; the launch traced here: 97.6 us
  Pallas kernels  89 us (91%)
  local copies, waits for them, and re-layouts  7.99 us (8%)
    pallas_call x1, Pallas kernels, body(): pl.pallas_call(functools.partial(kernel, n), out_shape=(jax.ShapeDtypeStr...  89 us
    unnamed x14, local copies, waits for them, and re-layouts  7.99 us

commit v1 on v0

--- a/solution.py
+++ b/solution.py
@@ -14,6 +14,7 @@
 DIFFUSION_RATE = 0.2
 OBJECT_STEP = 0.25
 EDGE = 8
+LANES = 128
 MESH = pl.DeviceIdType.MESH
 BF16 = jnp.bfloat16
 F32 = jnp.float32
@@ -56,13 +57,14 @@
     return real * weight, imag * weight
 
 
-def kernel(n, obj_ref, probe_ref, amp_ref, off_ref, cnt_ref, tab_ref, out_ref, pout_ref,
-           ext, pf, far, pw, pw_in, gext, patch, spill, ysend, yin, mar, ps, rbuf, po, ssem, rsem):
+def kernel(n, obj_in, probe_in, amp_in, off_ref, cnt_ref, tab_in, out_ref, pout_ref,
+           obj_ref, probe_ref, amp_ref, tab_ref, load_sem, ext, pf, far, pw, pw_in, gext, patch, spill, ysend, yin, mar, ps, rbuf, po, ssem, rsem):
     tile, columns = obj_ref.shape[1:]
     length = pf.shape[-1]
     slots, modes = pf.shape[0], probe_ref.shape[0]
     block = 2 * tile
     bits = n.bit_length() - 1
+    strips = length // LANES
     d, o = lax.axis_index("diff"), lax.axis_index("obj")
     q = 1 - o
     has_low, has_high = d > 0, d < n - 1
@@ -89,6 +91,11 @@
         near_at = lax.broadcasted_iota(jnp.int32, shape, 1 - long)
         return jnp.where(far_at - near_at == offset, 1.0, 0.0).astype(BF16)
 
+    loads = [pltpu.make_async_copy(src, dst, load_sem.at[i]) for i, (src, dst) in enumerate(
+        ((obj_in, obj_ref), (tab_in, tab_ref), (probe_in, probe_ref), (amp_in, amp_ref)))]
+    for load in loads:
+        load.start()
+
     barrier = pltpu.get_barrier_semaphore()
 
     def greet(device):
@@ -114,12 +121,14 @@
 
     to_partner, direct, relay = [], [], []
     for c in range(2):
-        to_partner.append(remote(obj_ref.at[c], ext.at[c, rows(o * tile, tile)], c, partner))
-        direct.append(remote(obj_ref.at[c], ext.at[c, rows(block + o * tile, tile)], 2 + c, lower))
+        to_partner.append(remote(obj_in.at[c], ext.at[c, rows(o * tile, tile)], c, partner))
+        direct.append(remote(obj_in.at[c], ext.at[c, rows(block + o * tile, tile)], 2 + c, lower))
         relay.append(remote(ext.at[c, rows(q * tile, tile)], ext.at[c, rows(block + q * tile, tile)], 4 + c, lower))
         to_partner[c].start()
     for c in range(2):
         pl.when(has_low)(direct[c].start)
+    for load in loads:
+        load.wait()
     for c in range(2):
         ext[c, rows(o * tile, tile), :] = obj_ref[c]
 
@@ -147,6 +156,33 @@
         pl.when(has_high)(direct[c].wait_recv)
     for c in range(2):
         pl.when(has_high)(relay[c].wait_recv)
+
+    base = 6 + slots
+    total = ps.shape[0] // modes
+    sums, shares, keeps, places = [], [], [], []
+    index = base + 5
+    for g in range(modes):
+        rest = list(range(1, bits))
+        turn = g % max(1, len(rest))
+        order = [0] + rest[turn:] + rest[:turn]
+        start, size, filled = g * total, total, g * total
+        sums.append([])
+        shares.append([])
+        keeps.append([])
+        places.append([])
+        for k in order:
+            half = size // 2
+            sums[g].append(remote(ps.at[rows(start + (1 - bit[k]) * half, half)],
+                                  rbuf.at[pl.ds(filled, half)], index, cube[k]))
+            places[g].append((filled, half))
+            start, size = start + bit[k] * half, half
+            keeps[g].append(rows(start, size))
+            filled += half
+            index += 1
+        for step, k in enumerate(order):
+            mine = po.at[keeps[g][step]]
+            shares[g].append(remote(mine, mine, index, cube[k]))
+            index += 1
 
     power_copy = []
     for s in range(slots):
@@ -170,7 +206,6 @@
         power_copy.append(remote(pw.at[s], pw_in.at[s], 6 + s, partner))
         power_copy[s].start()
 
-    base = 6 + slots
     for s in range(slots):
         used = jnp.full((1, length), cnt_ref[d], jnp.int32)
         weight = jnp.where(used > s, 1.0, 0.0).astype(F32)
@@ -190,15 +225,17 @@
             patch[1] += pr * imag - pi * real
             grad_r = fr * real + fi * imag
             grad_i = fr * imag - fi * real
-            at_r = rows(m * 2 * length, length)
-            at_i = rows(m * 2 * length + length, length)
-            if s == 0:
-                ps[at_r, :] = grad_r
-                ps[at_i, :] = grad_i
-            else:
-                ps[at_r, :] += grad_r
-                ps[at_i, :] += grad_i
-
+            for c, grad in ((0, grad_r), (1, grad_i)):
+                for h in range(strips):
+                    at = rows(((m * 2 + c) * strips + h) * length, length)
+                    if s == 0:
+                        ps[at, :] = grad[:, h * LANES:(h + 1) * LANES]
+                    else:
+                        ps[at, :] += grad[:, h * LANES:(h + 1) * LANES]
+
+        if s == slots - 1:
+            for g in range(modes):
+                sums[g][0].start()
         row_place = pick((2 * block, length), 0, off_ref[s, 0])
         column_place = pick((length, columns), 1, off_ref[s, 1])
         for c in range(2):
@@ -215,40 +252,23 @@
     for copy in spill_copy:
         pl.when(has_high)(copy.start)
 
-    sums_at, share_at = base + 5, base + 5 + bits
-    total = ps.shape[0]
-    starts, sizes = [jnp.int32(0)], [total]
-    sums, shares = [], []
-    filled = 0
-    for k in range(bits):
-        half = sizes[k] // 2
-        sums.append(remote(ps.at[rows(starts[k] + (1 - bit[k]) * half, half)], rbuf.at[pl.ds(filled, half)],
-                           sums_at + k, cube[k]))
-        starts.append(starts[k] + bit[k] * half)
-        sizes.append(half)
-        filled += half
-    for k in range(bits):
-        mine = po.at[rows(starts[k + 1], sizes[k + 1])]
-        shares.append(remote(mine, mine, share_at + k, cube[k]))
-
-    def add_sum(k):
-        sums[k].wait_recv()
-        at = total - sizes[k]
-        keep = rows(starts[k + 1], sizes[k + 1])
-        ps[keep, :] += rbuf[at:at + sizes[k + 1], :]
-
-    sums[0].start()
+    def add_sum(g, k):
+        sums[g][k].wait_recv()
+        at, size = places[g][k]
+        ps[keeps[g][k], :] += rbuf[at:at + size, :]
+
     pl.when(has_low)(spill_copy[0].wait_recv)
     ysend[...] = gext[:, rows(q * tile, tile), :] + spill[0]
     to_owner = remote(ysend, yin, base + 2, partner)
     to_owner.start()
     for k in range(bits):
-        add_sum(k)
-        if k + 1 < bits:
-            sums[k + 1].start()
-    last = rows(starts[bits], sizes[bits])
-    po[last, :] = ps[last, :]
-    shares[bits - 1].start()
+        for g in range(modes):
+            add_sum(g, k)
+            if k + 1 < bits:
+                sums[g][k + 1].start()
+            else:
+                po[keeps[g][k], :] = ps[keeps[g][k], :]
+                shares[g][k].start()
 
     pl.when(has_low)(spill_copy[1].wait_recv)
     to_owner.wait_recv()
@@ -262,9 +282,10 @@
     def share():
         if left:
             k = left.pop(0)
-            shares[k].wait_recv()
-            if left:
-                shares[left[0]].start()
+            for g in range(modes):
+                shares[g][k].wait_recv()
+                if left:
+                    shares[g][left[0]].start()
 
     share()
     pl.when(has_next)(up.wait_recv)
@@ -292,10 +313,12 @@
         share()
     for m in range(modes):
         for c in range(2):
-            at = (m * 2 + c) * length
-            pout_ref[m, c] = probe_ref[m, c] + po[at:at + length, :] / n
-
-    for copy in to_partner + power_copy + sums + shares + [to_owner]:
+            for h in range(strips):
+                at = ((m * 2 + c) * strips + h) * length
+                lanes = slice(h * LANES, (h + 1) * LANES)
+                pout_ref[m, c, :, lanes] = probe_ref[m, c, :, lanes] + po[at:at + length, :] / n
+
+    for copy in to_partner + power_copy + sum(sums, []) + sum(shares, []) + [to_owner]:
         copy.wait_send()
     for copy in direct + relay:
         pl.when(has_low)(copy.wait_send)
@@ -311,8 +334,9 @@
     slots = amplitudes.shape[0]
     bits = n.bit_length() - 1
     block = 2 * tile
-    copies = 11 + slots + 2 * bits
+    copies = 11 + slots + 2 * bits * modes
     vmem = pl.BlockSpec(memory_space=pltpu.VMEM)
+    hbm = pl.BlockSpec(memory_space=pltpu.HBM)
     smem = pl.BlockSpec(memory_space=pltpu.SMEM)
     tables = jnp.asarray(dft_blocks(length))
     return pl.pallas_call(
@@ -321,9 +345,14 @@
             jax.ShapeDtypeStruct(object_field.shape, F32),
             jax.ShapeDtypeStruct(probe_modes.shape, F32),
         ),
-        in_specs=[vmem, vmem, vmem, smem, smem, vmem],
+        in_specs=[hbm, hbm, hbm, smem, smem, hbm],
         out_specs=(vmem, vmem),
         scratch_shapes=[
+            pltpu.VMEM(object_field.shape, F32),
+            pltpu.VMEM(probe_modes.shape, F32),
+            pltpu.VMEM(amplitudes.shape, F32),
+            pltpu.VMEM(tables.shape, BF16),
+            pltpu.SemaphoreType.DMA((4,)),
             pltpu.VMEM((2, 2 * block, columns), F32),
             pltpu.VMEM((slots, 2, length, length), F32),
             pltpu.VMEM((slots, modes, length, 2 * length), F32),
@@ -335,9 +364,9 @@
             pltpu.VMEM((2, tile, columns), F32),
             pltpu.VMEM((2, tile, columns), F32),
             pltpu.VMEM((2, tile + 2 * EDGE, columns), F32),
-            pltpu.VMEM((modes * 2 * length, length), F32),
-            pltpu.VMEM((modes * 2 * length, length), F32),
-            pltpu.VMEM((modes * 2 * length, length), F32),
+            pltpu.VMEM((modes * 2 * length * length // LANES, LANES), F32),
+            pltpu.VMEM((modes * 2 * length * length // LANES, LANES), F32),
+            pltpu.VMEM((modes * 2 * length * length // LANES, LANES), F32),
             pltpu.SemaphoreType.DMA((copies,)),
             pltpu.SemaphoreType.DMA((copies,)),
         ],

time: 97.9 us -> 95.1 us (0.971)
  Pallas kernels: 89 us -> 86.2 us
    pallas_call x1, Pallas kernels: 89 us -> 86.2 us  [body(): pl.pallas_call(functools.partial(kernel, n), out_shape=(jax.ShapeDtypeStr...]
where the time goes in v1:
time: 95.1 us; the launch traced here: 94.8 us
  Pallas kernels  86.2 us (91%)
  local copies, waits for them, and re-layouts  7.99 us (8%)
    pallas_call x1, Pallas kernels, body(): pl.pallas_call(functools.partial(kernel, n), out_shape=(jax.ShapeDtypeStr...  86.2 us
    unnamed x14, local copies, waits for them, and re-layouts  7.99 us

profile of v1, /device:TPU:1, one launch (start us, length us, event | category | flops | bytes accessed | tf_op | source)
XLA Modules:
  0.0 94.8 jit_solution(17788343261011566195)
XLA Ops:
  0.6 0.0 copy-start
  0.6 1.6 %copy-done = bf16[2,2,512,512]{3,2,1,0:T(8,128)(2,1)S(1)} copy-done((bf16[2,2,512,512]{3,2,1,0:T(8,128)(2,1)S(1)}, bf16[2,2,512,512]{3,2,1,0:T(8,128)(2,1)}, u32[]{:S(2)}) %copy-start) | copy-done | bytes 2097176
  2.2 0.0 copy-start.1
  2.2 1.2 %copy-done.1 = f32[2,2,256,256]{3,2,1,0:T(8,128)S(1)} copy-done((f32[2,2,256,256]{3,2,1,0:T(8,128)S(1)}, f32[2,2,256,256]{3,2,1,0:T(8,128)}, u32[]{:S(2)}) %copy-start.1) | copy-done | bytes 1048600
  3.5 0.0 copy-start.2
  3.5 1.0 %copy-done.2 = f32[2,128,512]{2,1,0:T(8,128)S(1)} copy-done((f32[2,128,512]{2,1,0:T(8,128)S(1)}, f32[2,128,512]{2,1,0:T(8,128)}, u32[]{:S(2)}) %copy-start.2) | copy-done | bytes 524312
  4.5 0.0 copy-start.3
  4.5 1.0 %copy-done.3 = f32[2,256,256]{2,1,0:T(8,128)S(1)} copy-done((f32[2,256,256]{2,1,0:T(8,128)S(1)}, f32[2,256,256]{2,1,0:T(8,128)}, u32[]{:S(2)}) %copy-start.3) | copy-done | bytes 524312
  5.5 0.0 copy-start.4
  5.5 0.7 copy-done.4
  6.2 0.0 copy-start.5
  6.2 0.7 copy-done.5
  6.9 86.2 %shard_map.77 = (f32[2,128,512]{2,1,0:T(8,128)S(1)}, f32[2,2,256,256]{3,2,1,0:T(8,128)S(1)}) custom-call(f32[2,128,512]{2,1,0:T(8,128)S(1)} %copy-done.2, f32[2,2,256,256]{3,2,1,0:T(8,128)S(1)} %copy-done.1, f32[2,256,256]{2,1,0:T(8,128)S(1)} %copy-done.3, s32[2,2]{1,0:T(2,128)S(1)} %copy-done.4, s32[16]{0:T(128)S(1)} %copy-done.5, ...), custom_call_target="tpu_custom_call" | custom-call | tf_op jit(solution)/shard_map/pallas_call | solution.py:342
  93.0 0.8 copy.10
  93.8 1.0 %copy.11 = f32[2,2,256,256]{3,2,1,0:T(8,128)} copy(f32[2,2,256,256]{3,2,1,0:T(8,128)S(1)} %get-tuple-element.5) | data formatting | bytes 2097152
Async XLA Ops:
  0.6 1.6 %copy-start = (bf16[2,2,512,512]{3,2,1,0:T(8,128)(2,1)S(1)}, bf16[2,2,512,512]{3,2,1,0:T(8,128)(2,1)}, u32[]{:S(2)}) copy-start(bf16[2,2,512,512]{3,2,1,0:T(8,128)(2,1)} %constant.2.clone.tab_in) | copy-start | bytes 6291460
  2.2 1.2 %copy-start.1 = (f32[2,2,256,256]{3,2,1,0:T(8,128)S(1)}, f32[2,2,256,256]{3,2,1,0:T(8,128)}, u32[]{:S(2)}) copy-start(f32[2,2,256,256]{3,2,1,0:T(8,128)} %probe_in.1) | copy-start | bytes 3145732
  3.5 1.0 %copy-start.2 = (f32[2,128,512]{2,1,0:T(8,128)S(1)}, f32[2,128,512]{2,1,0:T(8,128)}, u32[]{:S(2)}) copy-start(f32[2,128,512]{2,1,0:T(8,128)} %obj_in.1) | copy-start | bytes 1572868
  4.5 1.0 %copy-start.3 = (f32[2,256,256]{2,1,0:T(8,128)S(1)}, f32[2,256,256]{2,1,0:T(8,128)}, u32[]{:S(2)}) copy-start(f32[2,256,256]{2,1,0:T(8,128)} %amp_in.1) | copy-start | bytes 1572868
  5.5 0.7 copy-start.4
  6.2 0.7 copy-start.5

commit v2 on v1

--- a/solution.py
+++ b/solution.py
@@ -58,7 +58,7 @@
 
 
 def kernel(n, obj_in, probe_in, amp_in, off_ref, cnt_ref, tab_in, out_ref, pout_ref,
-           obj_ref, probe_ref, amp_ref, tab_ref, load_sem, ext, pf, far, pw, pw_in, gext, patch, spill, ysend, yin, mar, ps, rbuf, po, ssem, rsem):
+           obj_ref, probe_ref, amp_ref, tab_ref, load_sem, cut, ext, pf, far, pw, pw_in, gext, patch, spill, ysend, yin, mar, ps, rbuf, po, ssem, rsem):
     tile, columns = obj_ref.shape[1:]
     length = pf.shape[-1]
     slots, modes = pf.shape[0], probe_ref.shape[0]
@@ -152,10 +152,19 @@
     for c in range(2):
         to_partner[c].wait_recv()
         pl.when(has_low)(relay[c].start)
+    def cut_columns(half):
+        for s in range(slots):
+            column_pick = pick((columns, length), 0, off_ref[s, 1])
+            for c in range(2):
+                high, low = split(ext[c, half * block:(half + 1) * block, :])
+                cut[s, c, half * block:(half + 1) * block, :] = dot(high, column_pick) + dot(low, column_pick)
+
+    cut_columns(0)
     for c in range(2):
         pl.when(has_high)(direct[c].wait_recv)
     for c in range(2):
         pl.when(has_high)(relay[c].wait_recv)
+    cut_columns(1)
 
     base = 6 + slots
     total = ps.shape[0] // modes
@@ -187,10 +196,8 @@
     power_copy = []
     for s in range(slots):
         row_pick = pick((length, 2 * block), 1, off_ref[s, 0])
-        column_pick = pick((columns, length), 0, off_ref[s, 1])
         for c in range(2):
-            high, low = split(ext[c])
-            high, low = split(dot(high, column_pick) + dot(low, column_pick))
+            high, low = split(cut[s, c])
             pf[s, c] = dot(row_pick, high) + dot(row_pick, low)
         pw[s] = jnp.zeros((length, length), F32)
 
@@ -233,9 +240,10 @@
                     else:
                         ps[at, :] += grad[:, h * LANES:(h + 1) * LANES]
 
-        if s == slots - 1:
-            for g in range(modes):
-                sums[g][0].start()
+            if s == slots - 1:
+                for g in range(modes):
+                    pl.when(m == g)(sums[g][0].start)
+
         row_place = pick((2 * block, length), 0, off_ref[s, 0])
         column_place = pick((length, columns), 1, off_ref[s, 1])
         for c in range(2):
@@ -353,6 +361,7 @@
             pltpu.VMEM(amplitudes.shape, F32),
             pltpu.VMEM(tables.shape, BF16),
             pltpu.SemaphoreType.DMA((4,)),
+            pltpu.VMEM((slots, 2, 2 * block, length), F32),
             pltpu.VMEM((2, 2 * block, columns), F32),
             pltpu.VMEM((slots, 2, length, length), F32),
             pltpu.VMEM((slots, modes, length, 2 * length), F32),

time: 95.1 us -> 93.9 us (0.987)
  Pallas kernels: 86.2 us -> 85 us
    pallas_call x1, Pallas kernels: 86.2 us -> 85 us  [body(): pl.pallas_call(functools.partial(kernel, n), out_shape=(jax.ShapeDtypeStr...]
where the time goes in v2:
time: 93.9 us; the launch traced here: 93.6 us
  Pallas kernels  85 us (91%)
  local copies, waits for them, and re-layouts  7.99 us (9%)
    pallas_call x1, Pallas kernels, body(): pl.pallas_call(functools.partial(kernel, n), out_shape=(jax.ShapeDtypeStr...  85 us
    unnamed x14, local copies, waits for them, and re-layouts  7.99 us

profile of v2, /device:TPU:1, one launch (start us, length us, event | category | flops | bytes accessed | tf_op | source)
XLA Modules:
  0.0 93.6 jit_solution(14789834270493561460)
XLA Ops:
  0.6 0.0 copy-start
  0.6 1.6 %copy-done = bf16[2,2,512,512]{3,2,1,0:T(8,128)(2,1)S(1)} copy-done((bf16[2,2,512,512]{3,2,1,0:T(8,128)(2,1)S(1)}, bf16[2,2,512,512]{3,2,1,0:T(8,128)(2,1)}, u32[]{:S(2)}) %copy-start) | copy-done | bytes 2097176
  2.2 0.0 copy-start.1
  2.2 1.2 %copy-done.1 = f32[2,2,256,256]{3,2,1,0:T(8,128)S(1)} copy-done((f32[2,2,256,256]{3,2,1,0:T(8,128)S(1)}, f32[2,2,256,256]{3,2,1,0:T(8,128)}, u32[]{:S(2)}) %copy-start.1) | copy-done | bytes 1048600
  3.5 0.0 copy-start.2
  3.5 1.0 %copy-done.2 = f32[2,128,512]{2,1,0:T(8,128)S(1)} copy-done((f32[2,128,512]{2,1,0:T(8,128)S(1)}, f32[2,128,512]{2,1,0:T(8,128)}, u32[]{:S(2)}) %copy-start.2) | copy-done | bytes 524312
  4.5 0.0 copy-start.3
  4.5 1.0 %copy-done.3 = f32[2,256,256]{2,1,0:T(8,128)S(1)} copy-done((f32[2,256,256]{2,1,0:T(8,128)S(1)}, f32[2,256,256]{2,1,0:T(8,128)}, u32[]{:S(2)}) %copy-start.3) | copy-done | bytes 524312
  5.5 0.0 copy-start.4
  5.5 0.7 copy-done.4
  6.2 0.0 copy-start.5
  6.2 0.7 copy-done.5
  6.9 85.0 %shard_map.77 = (f32[2,128,512]{2,1,0:T(8,128)S(1)}, f32[2,2,256,256]{3,2,1,0:T(8,128)S(1)}) custom-call(f32[2,128,512]{2,1,0:T(8,128)S(1)} %copy-done.2, f32[2,2,256,256]{3,2,1,0:T(8,128)S(1)} %copy-done.1, f32[2,256,256]{2,1,0:T(8,128)S(1)} %copy-done.3, s32[2,2]{1,0:T(2,128)S(1)} %copy-done.4, s32[16]{0:T(128)S(1)} %copy-done.5, ...), custom_call_target="tpu_custom_call" | custom-call | tf_op jit(solution)/shard_map/pallas_call | solution.py:350
  91.9 0.8 copy.10
  92.7 1.0 %copy.11 = f32[2,2,256,256]{3,2,1,0:T(8,128)} copy(f32[2,2,256,256]{3,2,1,0:T(8,128)S(1)} %get-tuple-element.5) | data formatting | bytes 2097152
Async XLA Ops:
  0.6 1.6 %copy-start = (bf16[2,2,512,512]{3,2,1,0:T(8,128)(2,1)S(1)}, bf16[2,2,512,512]{3,2,1,0:T(8,128)(2,1)}, u32[]{:S(2)}) copy-start(bf16[2,2,512,512]{3,2,1,0:T(8,128)(2,1)} %constant.2.clone.tab_in) | copy-start | bytes 6291460
  2.2 1.2 %copy-start.1 = (f32[2,2,256,256]{3,2,1,0:T(8,128)S(1)}, f32[2,2,256,256]{3,2,1,0:T(8,128)}, u32[]{:S(2)}) copy-start(f32[2,2,256,256]{3,2,1,0:T(8,128)} %probe_in.1) | copy-start | bytes 3145732
  3.5 1.0 %copy-start.2 = (f32[2,128,512]{2,1,0:T(8,128)S(1)}, f32[2,128,512]{2,1,0:T(8,128)}, u32[]{:S(2)}) copy-start(f32[2,128,512]{2,1,0:T(8,128)} %obj_in.1) | copy-start | bytes 1572868
  4.5 1.0 %copy-start.3 = (f32[2,256,256]{2,1,0:T(8,128)S(1)}, f32[2,256,256]{2,1,0:T(8,128)}, u32[]{:S(2)}) copy-start(f32[2,256,256]{2,1,0:T(8,128)} %amp_in.1) | copy-start | bytes 1572868
  5.5 0.7 copy-start.4
  6.2 0.7 copy-start.5

commit v3 on v2

--- a/solution.py
+++ b/solution.py
@@ -257,18 +257,14 @@
 
     spill_copy = [remote(gext.at[:, rows(block + t * tile, tile)], spill.at[h], base + h, upper)
                   for h, t in ((0, q), (1, o))]
-    for copy in spill_copy:
-        pl.when(has_high)(copy.start)
+    pl.when(has_high)(spill_copy[0].start)
 
     def add_sum(g, k):
         sums[g][k].wait_recv()
         at, size = places[g][k]
         ps[keeps[g][k], :] += rbuf[at:at + size, :]
 
-    pl.when(has_low)(spill_copy[0].wait_recv)
-    ysend[...] = gext[:, rows(q * tile, tile), :] + spill[0]
     to_owner = remote(ysend, yin, base + 2, partner)
-    to_owner.start()
     for k in range(bits):
         for g in range(modes):
             add_sum(g, k)
@@ -277,6 +273,11 @@
             else:
                 po[keeps[g][k], :] = ps[keeps[g][k], :]
                 shares[g][k].start()
+        if k == 0:
+            pl.when(has_high)(spill_copy[1].start)
+            pl.when(has_low)(spill_copy[0].wait_recv)
+            ysend[...] = gext[:, rows(q * tile, tile), :] + spill[0]
+            to_owner.start()
 
     pl.when(has_low)(spill_copy[1].wait_recv)
     to_owner.wait_recv()

time: 93.9 us -> 89.7 us (0.955)
  the two profiles are of different devices: /device:TPU:1 before, /device:TPU:7 now
where the time goes in v3:
time: 89.7 us; the launch traced here: 89.4 us
  Pallas kernels  80.7 us (90%)
  local copies, waits for them, and re-layouts  7.99 us (9%)
    pallas_call x1, Pallas kernels, body(): pl.pallas_call(functools.partial(kernel, n), out_shape=(jax.ShapeDtypeStr...  80.7 us
    unnamed x14, local copies, waits for them, and re-layouts  7.99 us

profile of v3, /device:TPU:7, one launch (start us, length us, event | category | flops | bytes accessed | tf_op | source)
XLA Modules:
  0.0 89.4 jit_solution(13867259378538540050)
XLA Ops:
  0.6 0.0 copy-start
  0.6 1.6 %copy-done = bf16[2,2,512,512]{3,2,1,0:T(8,128)(2,1)S(1)} copy-done((bf16[2,2,512,512]{3,2,1,0:T(8,128)(2,1)S(1)}, bf16[2,2,512,512]{3,2,1,0:T(8,128)(2,1)}, u32[]{:S(2)}) %copy-start) | copy-done | bytes 2097176
  2.2 0.0 copy-start.1
  2.2 1.2 %copy-done.1 = f32[2,2,256,256]{3,2,1,0:T(8,128)S(1)} copy-done((f32[2,2,256,256]{3,2,1,0:T(8,128)S(1)}, f32[2,2,256,256]{3,2,1,0:T(8,128)}, u32[]{:S(2)}) %copy-start.1) | copy-done | bytes 1048600
  3.5 0.0 copy-start.2
  3.5 1.0 %copy-done.2 = f32[2,128,512]{2,1,0:T(8,128)S(1)} copy-done((f32[2,128,512]{2,1,0:T(8,128)S(1)}, f32[2,128,512]{2,1,0:T(8,128)}, u32[]{:S(2)}) %copy-start.2) | copy-done | bytes 524312
  4.5 0.0 copy-start.3
  4.5 1.0 %copy-done.3 = f32[2,256,256]{2,1,0:T(8,128)S(1)} copy-done((f32[2,256,256]{2,1,0:T(8,128)S(1)}, f32[2,256,256]{2,1,0:T(8,128)}, u32[]{:S(2)}) %copy-start.3) | copy-done | bytes 524312
  5.5 0.0 copy-start.4
  5.5 0.7 copy-done.4
  6.2 0.0 copy-start.5
  6.2 0.7 copy-done.5
  6.9 80.7 %shard_map.77 = (f32[2,128,512]{2,1,0:T(8,128)S(1)}, f32[2,2,256,256]{3,2,1,0:T(8,128)S(1)}) custom-call(f32[2,128,512]{2,1,0:T(8,128)S(1)} %copy-done.2, f32[2,2,256,256]{3,2,1,0:T(8,128)S(1)} %copy-done.1, f32[2,256,256]{2,1,0:T(8,128)S(1)} %copy-done.3, s32[2,2]{1,0:T(2,128)S(1)} %copy-done.4, s32[16]{0:T(128)S(1)} %copy-done.5, ...), custom_call_target="tpu_custom_call" | custom-call | tf_op jit(solution)/shard_map/pallas_call | solution.py:351
  87.6 0.8 copy.10
  88.4 1.0 %copy.11 = f32[2,2,256,256]{3,2,1,0:T(8,128)} copy(f32[2,2,256,256]{3,2,1,0:T(8,128)S(1)} %get-tuple-element.5) | data formatting | bytes 2097152
Async XLA Ops:
  0.6 1.6 %copy-start = (bf16[2,2,512,512]{3,2,1,0:T(8,128)(2,1)S(1)}, bf16[2,2,512,512]{3,2,1,0:T(8,128)(2,1)}, u32[]{:S(2)}) copy-start(bf16[2,2,512,512]{3,2,1,0:T(8,128)(2,1)} %constant.2.clone.tab_in) | copy-start | bytes 6291460
  2.2 1.2 %copy-start.1 = (f32[2,2,256,256]{3,2,1,0:T(8,128)S(1)}, f32[2,2,256,256]{3,2,1,0:T(8,128)}, u32[]{:S(2)}) copy-start(f32[2,2,256,256]{3,2,1,0:T(8,128)} %probe_in.1) | copy-start | bytes 3145732
  3.5 1.0 %copy-start.2 = (f32[2,128,512]{2,1,0:T(8,128)S(1)}, f32[2,128,512]{2,1,0:T(8,128)}, u32[]{:S(2)}) copy-start(f32[2,128,512]{2,1,0:T(8,128)} %obj_in.1) | copy-start | bytes 1572868
  4.5 1.0 %copy-start.3 = (f32[2,256,256]{2,1,0:T(8,128)S(1)}, f32[2,256,256]{2,1,0:T(8,128)}, u32[]{:S(2)}) copy-start(f32[2,256,256]{2,1,0:T(8,128)} %amp_in.1) | copy-start | bytes 1572868
  5.5 0.7 copy-start.4
  6.2 0.7 copy-start.5
